TPU v7x, 512 devices: a whole 4x4x16 slice. The times are simulated.
512 devices in a mesh: dp: 32 (over z, core), tensor: 16 (over y, x).
Axes of the slice: x: 4, y: 4, z: 16, core: 2. Of those that a mesh axis runs over, the one named last changes fastest.
Arguments:
- hidden: bfloat16 [8192, 4096], P(('dp', 'tensor')), may hold values from -3.6 to 3.6
- lengths: int32 [32, 32], P('dp'), may hold values from 1 to 80, 256 in all within a row
- positives: int32 [256], replicated, may hold values from 0 to 767, as said below
- negatives: int32 [256, 7], replicated, may hold values from 1 to 766, as said below
- in_gain: float32 [4096], replicated, may hold values from 0.25 to 1.75
- wq: bfloat16 [4096, 2048], P(None, 'tensor'), may hold values from -0.09375 to 0.09375
- wkv: bfloat16 [4096, 2048], P(None, 'tensor'), may hold values from -0.09375 to 0.09375
- q_gain: float32 [128], replicated, may hold values from 0.25 to 1.75
- k_gain: float32 [128], replicated, may hold values from 0.25 to 1.75
- wo: bfloat16 [2048, 4096], P('tensor'), may hold values from -0.125 to 0.125
- out_gain: float32 [4096], replicated, may hold values from 0.25 to 1.75
Outputs:
- d_hidden: bfloat16 [8192, 4096], P(('dp', 'tensor'))
- loss: float32 [], replicated
Inputs may be any that keep to these rules, and one draw needn't show every extreme that they name: Each group's 32 lengths sum to 256, and one of them is exactly 80. The 256 positives are distinct passages. The 7 hard negatives of a query are distinct, and none of them is any query's positive.
All inputs are finite; a program needn't handle non-finite values.
Results may differ from a plain program's by a relative error of at most 0.023.
Values may be sent and summed in bfloat16 or wider, within the bound.
No kernel may reach another device: no remote copies, remote signals or barrier semaphores. Data moves between devices by JAX's collectives and lax.ppermute only.
A program may use at most 64 MiB of HBM per device.

v0:
```python
import math
import jax
import jax.numpy as jnp
from jax import lax
from jax.sharding import PartitionSpec as P

QDEV = 8
EPSILON = 1e-06
SOFTMAX_TEMPER = 0.05
LOSS_MULTIPLIER = 8192.0
ROPE_BASE = 1000000.0


def swapped(value, axis, apart):
    mask = 2**apart
    pairs = [(source, source ^ mask) for source in range(lax.axis_size(axis))]
    return lax.ppermute(value, axis, pairs)


def rms_scale(tensor):
    return lax.rsqrt(jnp.mean(tensor * tensor, axis=-1, keepdims=True) + EPSILON)


def rope_tables(position, head_width):
    halfway = head_width // 2
    frequency = ROPE_BASE ** (-(jnp.arange(halfway, dtype=jnp.float32) * (2.0 / head_width)))
    angles = position[:, None] * frequency[None, :]
    angles = jnp.concatenate([angles, angles], axis=-1)
    return (jnp.cos(angles), jnp.sin(angles))


def rotate(tensor, cosine, sine):
    halfway = tensor.shape[-1] // 2
    turned = jnp.concatenate([-tensor[..., halfway:], tensor[..., :halfway]], axis=-1)
    return tensor * cosine + turned * sine


def segment_layout(lengths_row, total_tokens):
    seq_ends = jnp.cumsum(lengths_row)
    starts = seq_ends - lengths_row
    token_index = jnp.arange(total_tokens, dtype=jnp.int32)
    inside = (token_index[:, None] >= starts[None, :]) & (token_index[:, None] < seq_ends[None, :])
    offset = jnp.sum(jnp.where(inside, starts[None, :], 0), axis=1)
    position = (token_index - offset).astype(jnp.float32)
    return (inside, position, seq_ends - 1)


def head_forward(raw, gain, cosine, sine):
    inverse = rms_scale(raw)
    unit_form = raw * inverse
    return (unit_form, inverse, rotate(unit_form * gain, cosine, sine))


def norm_backward(grad, unit_form, inverse, gain):
    scaled = grad * gain
    return inverse * (scaled - unit_form * jnp.mean(unit_form * scaled, axis=-1, keepdims=True))


def head_backward(grad_rot, unit_form, inverse, gain, cosine, sine):
    return norm_backward(rotate(grad_rot, cosine, -sine), unit_form, inverse, gain)


def exchange(blocks, axis):
    return lax.all_to_all(blocks, axis, 0, 0, tiled=True)


def gather_rows(rows, axis):
    count = lax.axis_size(axis)
    copies = jnp.broadcast_to(rows[None], (count,) + rows.shape)
    return exchange(copies, axis)


def to_lanes(block, lanes):
    rows, width = block.shape
    return block.reshape(rows, width // lanes, lanes).reshape(-1, lanes)


def split16(value):
    parts = []
    rest = value
    for _ in range(3):
        part = rest.astype(jnp.bfloat16)
        parts.append(part)
        rest = rest - part.astype(jnp.float32)
    return parts


def contrast(scaled16, out_gain, positives, negatives):
    groups, sequences, width = scaled16.shape
    tensor_count = lax.axis_size("tensor")
    query_rows = scaled16[:, :QDEV].reshape(groups * QDEV, width)
    passage_rows = scaled16[:, QDEV:].reshape(-1, width)
    query_count, passage_count = (query_rows.shape[0], passage_rows.shape[0])
    own_queries = query_count // tensor_count
    features = width * tensor_count
    raw = jnp.dot(query_rows, passage_rows.T, preferred_element_type=jnp.float32)
    rows32 = jnp.concatenate([query_rows, passage_rows]).astype(jnp.float32)
    plain = rows32 / out_gain
    squares = jnp.sum(rows32 * rows32 + plain * plain * (EPSILON / features), axis=1)
    lanes = 128
    logit_rows = own_queries * passage_count // lanes
    packed = jnp.concatenate(
        [
            raw.reshape(tensor_count, own_queries, passage_count // lanes, lanes).reshape(
                tensor_count, logit_rows, lanes
            ),
            jnp.broadcast_to(
                squares.reshape(1, -1, lanes), (tensor_count, squares.shape[0] // lanes, lanes)
            ),
        ],
        axis=1,
    )
    summed = jnp.sum(exchange(packed, "tensor"), axis=0)
    inverse = lax.rsqrt(summed[logit_rows:].reshape(-1) + EPSILON * EPSILON)
    own = lax.axis_index("tensor") * own_queries
    inverse_query = lax.dynamic_slice_in_dim(inverse[:query_count], own, own_queries)
    inverse_passage = inverse[query_count:]
    logits = (
        summed[:logit_rows].reshape(own_queries, passage_count)
        * inverse_query[:, None]
        * inverse_passage[None, :]
        / SOFTMAX_TEMPER
    )
    passage_ids = jnp.arange(passage_count, dtype=jnp.int32)
    any_positive = jnp.any(positives[:, None] == passage_ids[None, :], axis=0)
    own_positives = lax.dynamic_slice_in_dim(positives, own, own_queries)
    own_negatives = lax.dynamic_slice_in_dim(negatives, own, own_queries)
    positive_hot = own_positives[:, None] == passage_ids[None, :]
    hard_hot = jnp.any(own_negatives[:, :, None] == passage_ids[None, None, :], axis=1)
    permitted_mask = any_positive[None, :] | hard_hot
    weight_params = jnp.where(permitted_mask, jnp.exp(logits - 1.0 / SOFTMAX_TEMPER), 0.0)
    totals = jnp.sum(weight_params, axis=1, keepdims=True)
    target_labels = jnp.sum(jnp.where(positive_hot, logits, 0.0), axis=1)
    loss_part = jnp.sum(jnp.log(totals[:, 0]) + 1.0 / SOFTMAX_TEMPER - target_labels)
    scaling_factor = LOSS_MULTIPLIER / (query_count * SOFTMAX_TEMPER)
    coef16 = (scaling_factor * (weight_params / totals - positive_hot.astype(jnp.float32))).astype(
        jnp.bfloat16
    )
    weighted = coef16.astype(jnp.float32) * logits * SOFTMAX_TEMPER
    along_query = jnp.sum(weighted, axis=1)
    along_passage = jnp.sum(weighted, axis=0)
    small = jnp.concatenate(
        [
            along_passage,
            jnp.pad(jnp.concatenate([along_query, loss_part[None]]), (0, lanes - own_queries - 1)),
        ]
    ).reshape(-1, lanes)
    small_rows = small.shape[0]
    sent = jnp.concatenate([coef16.reshape(-1, lanes)] + split16(small))
    pad = -sent.shape[0] % 16
    sent = jnp.pad(sent, ((0, pad), (0, 0)))
    arrived = gather_rows(sent, "tensor").reshape(tensor_count, -1, lanes)
    coef_all = arrived[:, :logit_rows].reshape(query_count, passage_count)
    parts = arrived[:, logit_rows : logit_rows + 3 * small_rows].astype(jnp.float32)
    small_all = jnp.sum(parts.reshape(tensor_count, 3, small_rows, lanes), axis=1)
    along_passage = jnp.sum(small_all[:, : small_rows - 1], axis=0).reshape(-1)
    along_query = small_all[:, small_rows - 1, :own_queries].reshape(-1)
    loss = jnp.sum(small_all[:, small_rows - 1, own_queries]) / query_count
    embeds16 = (rows32 * inverse[:, None]).astype(jnp.bfloat16)
    d_queries = jnp.dot(coef_all, embeds16[query_count:], preferred_element_type=jnp.float32)
    d_passages = jnp.dot(coef_all.T, embeds16[:query_count], preferred_element_type=jnp.float32)
    own_group = lax.axis_index("dp")
    others = sequences - QDEV

    def own_part(of_queries, of_passages):
        return jnp.concatenate(
            [
                lax.dynamic_slice_in_dim(of_queries, own_group * QDEV, QDEV),
                lax.dynamic_slice_in_dim(of_passages, own_group * others, others),
            ]
        )

    return (
        loss,
        own_part(d_queries, d_passages),
        own_part(along_query, along_passage),
        own_part(inverse[:query_count], inverse_passage),
    )


def on_device(
    hidden, lengths, positives, negatives, in_gain, wq, wkv, q_gain, k_gain, wo, out_gain
):
    tensor_count = lax.axis_size("tensor")
    tensor_index = lax.axis_index("tensor")
    own_rows, features = hidden.shape
    tokens_count = own_rows * tensor_count
    head_width = wq.shape[1]
    sequences = lengths.shape[1]
    chunk = features // tensor_count
    root = math.sqrt(head_width)
    is_even = tensor_index % 2 == 0
    hidden32 = hidden.astype(jnp.float32)
    inverse_in = rms_scale(hidden32)
    normed = (hidden32 * inverse_in * in_gain).astype(jnp.bfloat16)
    piece = gather_rows(normed, "tensor").reshape(tokens_count, features)
    own_index = tensor_index * own_rows + jnp.arange(own_rows, dtype=jnp.int32)
    inside, position, last = segment_layout(lengths[0], tokens_count)
    own_last = (last[:, None] == own_index[None, :]).astype(jnp.bfloat16)
    token_index = jnp.arange(tokens_count, dtype=jnp.int32)
    chosen = (last[:, None] == token_index[None, :]).astype(jnp.bfloat16)
    kv_own = jnp.dot(piece, wkv, preferred_element_type=jnp.float32)
    kv_other = swapped(kv_own, "tensor", 0)
    last_rows = jnp.dot(chosen, piece, preferred_element_type=jnp.float32).astype(jnp.bfloat16)
    query_raw = jnp.dot(last_rows, wq, preferred_element_type=jnp.float32)
    key_raw = jnp.where(is_even, kv_own, kv_other)
    value16 = jnp.where(is_even, kv_other, kv_own).astype(jnp.bfloat16)
    cos_key, sin_key = rope_tables(position, head_width)
    key_unit, key_inverse, key_rot = head_forward(key_raw, k_gain, cos_key, sin_key)
    key16 = key_rot.astype(jnp.bfloat16)
    cos_query, sin_query = rope_tables((lengths[0] - 1).astype(jnp.float32), head_width)
    query_unit, query_inverse, query_rot = head_forward(query_raw, q_gain, cos_query, sin_query)
    query16 = query_rot.astype(jnp.bfloat16)
    shift = root * jnp.max(q_gain) * jnp.max(k_gain)
    scores = jnp.dot(query16, key16.T, preferred_element_type=jnp.float32) / root
    weight_params = jnp.where(inside.T, jnp.exp(scores - shift), 0.0)
    probs = weight_params / jnp.sum(weight_params, axis=-1, keepdims=True)
    probs16 = probs.astype(jnp.bfloat16)
    attn16 = jnp.dot(probs16, value16, preferred_element_type=jnp.float32).astype(jnp.bfloat16)
    partial_rows = jnp.dot(attn16, wo, preferred_element_type=jnp.float32) + jnp.dot(
        own_last, hidden, preferred_element_type=jnp.float32
    )
    blocks = partial_rows.astype(jnp.bfloat16).reshape(sequences, tensor_count, chunk)
    arrived = exchange(blocks.transpose(1, 0, 2), "tensor")
    resid = jnp.sum(arrived.astype(jnp.float32), axis=0)
    own_gain = lax.dynamic_slice_in_dim(out_gain, tensor_index * chunk, chunk)
    scaled = resid * own_gain
    everyone = lax.all_gather(scaled.astype(jnp.bfloat16), "dp", axis=0, tiled=True)
    groups = lax.axis_size("dp")
    loss, d_embed, along, inverse = contrast(
        everyone.reshape(groups, sequences, chunk), own_gain, positives, negatives
    )
    inverse, along = (inverse[:, None], along[:, None])
    d_resid = inverse * own_gain * (d_embed - scaled * inverse * along) - resid * (
        along * inverse * inverse * (EPSILON / features)
    )
    d_resid16 = gather_rows(d_resid.astype(jnp.bfloat16), "tensor")
    d_resid16 = d_resid16.reshape(tensor_count, sequences, chunk)
    d_resid16 = d_resid16.transpose(1, 0, 2).reshape(sequences, features)
    d_attn16 = jnp.dot(d_resid16, wo.T, preferred_element_type=jnp.float32).astype(jnp.bfloat16)
    d_probs = jnp.dot(d_attn16, value16.T, preferred_element_type=jnp.float32)
    d_scores16 = (
        probs * (d_probs - jnp.sum(probs * d_probs, axis=-1, keepdims=True)) / root
    ).astype(jnp.bfloat16)
    d_query_rot = jnp.dot(d_scores16, key16, preferred_element_type=jnp.float32)
    d_key_rot = jnp.dot(d_scores16.T, query16, preferred_element_type=jnp.float32)
    d_value = jnp.dot(probs16.T, d_attn16, preferred_element_type=jnp.float32)
    d_key_raw = head_backward(d_key_rot, key_unit, key_inverse, k_gain, cos_key, sin_key)
    d_query_raw = head_backward(
        d_query_rot, query_unit, query_inverse, q_gain, cos_query, sin_query
    )
    mine = jnp.where(is_even, d_key_raw, d_value)
    theirs = jnp.where(is_even, d_value, d_key_raw)
    column16 = (mine + swapped(theirs, "tensor", 0)).astype(jnp.bfloat16)
    spread16 = jnp.dot(
        chosen.T, d_query_raw.astype(jnp.bfloat16), preferred_element_type=jnp.float32
    ).astype(jnp.bfloat16)
    product = jnp.dot(column16, wkv.T, preferred_element_type=jnp.float32) + jnp.dot(
        spread16, wq.T, preferred_element_type=jnp.float32
    )
    terms = exchange(product.astype(jnp.bfloat16), "tensor")
    d_normed = jnp.sum(terms.reshape(tensor_count, own_rows, features).astype(jnp.float32), axis=0)
    d_hidden = norm_backward(d_normed, hidden32 * inverse_in, inverse_in, in_gain)
    d_hidden = d_hidden + jnp.dot(own_last.T, d_resid16, preferred_element_type=jnp.float32)
    return (d_hidden.astype(jnp.bfloat16), loss)


def solution(mesh):
    placed = (
        P(("dp", "tensor"), None),
        P("dp", None),
        P(),
        P(),
        P(),
        P(None, "tensor"),
        P(None, "tensor"),
        P(),
        P(),
        P("tensor", None),
        P(),
    )
    return jax.shard_map(
        on_device,
        mesh=mesh,
        in_specs=placed,
        out_specs=(P(("dp", "tensor"), None), P()),
        check_vma=False,
    )
```

profile of v0, /device:TPU:2, one launch (start us, length us, event | category | flops | bytes accessed | tf_op | source)
XLA Modules:
  0.0 216.7 jit_solution(15755054820013921453)
XLA Ops:
  0.6 1.1 fusion.24
  2.3 1.0 fusion.20
  3.3 1.6 broadcast_in_dim.31
  4.9 9.6 %all-to-all-start = ((bf16[16,16,4096]{2,1,0:T(8,128)(2,1)}), bf16[16,16,4096]{2,1,0:T(8,128)(2,1)S(1)}, u32[]{:S(2)}, u32[]{:S(2)}) async-start(bf16[16,16,4096]{2,1,0:T(8,128)(2,1)} %broadcast_in_dim.31), calls=%async_computation | async-start | bytes 4194304 | tf_op jit(solution)/shard_map/all_to_all | solution.py:64
  17.5 1.1 fusion.53
  18.6 21.2 %all-to-all-done = bf16[16,16,4096]{2,1,0:T(8,128)(2,1)S(1)} async-done(((bf16[16,16,4096]{2,1,0:T(8,128)(2,1)}), bf16[16,16,4096]{2,1,0:T(8,128)(2,1)S(1)}, u32[]{:S(2)}, u32[]{:S(2)}) %all-to-all-start) | async-done | bytes 2097184 | tf_op jit(solution)/shard_map/all_to_all | solution.py:64
  39.8 2.0 multiply_reduce_fusion.6
  42.7 4.8 %collective-permute-start = (f32[256,128]{0,1:T(8,128)S(1)}, f32[256,128]{0,1:T(8,128)S(1)}, u32[]{:S(2)}, u32[]{:S(2)}) collective-permute-start(f32[256,128]{0,1:T(8,128)S(1)} %fusion.88), channel_id=1, source_target_pairs={{0,1},{1,0},{2,3},{3,2},{4,5},{5,4},{6,7},{7,6},{8,9},{9,8},{10,11... | collective-permute-start | bytes 393224 | tf_op jit(solution)/shard_map/ppermute | solution.py:17
  47.8 2.6 %collective-permute-done = f32[256,128]{0,1:T(8,128)S(1)} collective-permute-done((f32[256,128]{0,1:T(8,128)S(1)}, f32[256,128]{0,1:T(8,128)S(1)}, u32[]{:S(2)}, u32[]{:S(2)}) %collective-permute-start) | collective-permute-done | bytes 131104 | tf_op jit(solution)/shard_map/ppermute | solution.py:17
  53.3 5.3 %all-to-all-start.1 = ((bf16[16,32,256]{2,1,0:T(8,128)(2,1)}), bf16[16,32,256]{2,1,0:T(8,128)(2,1)S(1)}, u32[]{:S(2)}, u32[]{:S(2)}) async-start(bf16[16,32,256]{2,1,0:T(8,128)(2,1)} %bitcast.79), calls=%async_computation.1 | async-start | bytes 524288 | tf_op jit(solution)/shard_map/all_to_all | solution.py:64
  59.4 6.7 %all-to-all-done.1 = bf16[16,32,256]{2,1,0:T(8,128)(2,1)S(1)} async-done(((bf16[16,32,256]{2,1,0:T(8,128)(2,1)}), bf16[16,32,256]{2,1,0:T(8,128)(2,1)S(1)}, u32[]{:S(2)}, u32[]{:S(2)}) %all-to-all-start.1) | async-done | bytes 262176 | tf_op jit(solution)/shard_map/all_to_all | solution.py:64
  66.1 39.5 %all_gather.3 = bf16[1024,256]{1,0:T(8,128)(2,1)S(1)} all-gather(bf16[32,256]{1,0:T(8,128)(2,1)S(1)} %multiply_convert_fusion.3), channel_id=1, replica_groups=mesh['dp'=32,'tensor'=16] {'dp'}, dimensions={0}, use_global_device_ids=true | all-gather | bytes 540672 | tf_op jit(solution)/shard_map/all_gather | solution.py:228
  106.5 0.9 reshape_reshape.3
  107.5 2.1 pad_maximum_fusion
  109.6 4.9 %all-to-all-start.2 = ((f32[16,104,128]{2,1,0:T(8,128)}), f32[16,104,128]{2,1,0:T(8,128)S(1)}, u32[]{:S(2)}, u32[]{:S(2)}) async-start(f32[16,104,128]{2,1,0:T(8,128)} %pad_maximum_fusion), calls=%async_computation.2 | async-start | bytes 1703936 | tf_op jit(solution)/shard_map/all_to_all | solution.py:64
  117.6 11.6 %all-to-all-done.2 = f32[16,104,128]{2,1,0:T(8,128)S(1)} async-done(((f32[16,104,128]{2,1,0:T(8,128)}), f32[16,104,128]{2,1,0:T(8,128)S(1)}, u32[]{:S(2)}, u32[]{:S(2)}) %all-to-all-start.2) | async-done | bytes 852000 | tf_op jit(solution)/shard_map/all_to_all | solution.py:64
  129.5 0.9 fusion.51
  130.9 1.0 multiply_reduce_fusion.2
  134.5 0.9 broadcast_in_dim.40
  135.5 5.6 %all-to-all-start.3 = ((bf16[16,128,128]{2,1,0:T(8,128)(2,1)}), bf16[16,128,128]{2,1,0:T(8,128)(2,1)}, u32[]{:S(2)}, u32[]{:S(2)}) async-start(bf16[16,128,128]{2,1,0:T(8,128)(2,1)} %broadcast_in_dim.40), calls=%async_computation.3 | async-start | bytes 1048576 | tf_op jit(solution)/shard_map/all_to_all | solution.py:64
  142.5 8.9 %all-to-all-done.3 = bf16[16,128,128]{2,1,0:T(8,128)(2,1)} async-done(((bf16[16,128,128]{2,1,0:T(8,128)(2,1)}), bf16[16,128,128]{2,1,0:T(8,128)(2,1)}, u32[]{:S(2)}, u32[]{:S(2)}) %all-to-all-start.3) | async-done | bytes 524320 | tf_op jit(solution)/shard_map/all_to_all | solution.py:64
  151.4 0.9 slice.105
  153.6 1.0 slice.102
  155.3 1.2 fusion.25
  158.5 11.6 %all_to_all.34 = bf16[16,32,256]{2,1,0:T(8,128)(2,1)S(1)} all-to-all(bf16[16,32,256]{2,1,0:T(8,128)(2,1)S(1)} %broadcast_in_dim.41), channel_id=1, replica_groups=mesh['dp'=32,'tensor'=16] {'tensor'}, dimensions={0} | all-to-all | bytes 524288 | tf_op jit(solution)/shard_map/all_to_all | solution.py:64
  172.5 3.4 %collective-permute-start.1 = (f32[256,128]{0,1:T(8,128)S(1)}, f32[256,128]{0,1:T(8,128)S(1)}, u32[]{:S(2)}, u32[]{:S(2)}) collective-permute-start(f32[256,128]{0,1:T(8,128)S(1)} %get-tuple-element.39), channel_id=1, source_target_pairs={{0,1},{1,0},{2,3},{3,2},{4,5},{5,4},{6,7},{7,6},{8,9},{9,8},{10,11... | collective-permute-start | bytes 393224 | tf_op jit(solution)/shard_map/ppermute | solution.py:17
  175.9 4.1 %fusion.4 = f32[256,4096]{1,0:T(8,128)} fusion(bf16[4096,128]{1,0:T(8,128)(2,1)} %param.16, s32[32]{0:T(128)S(1)} %copy-done.31, f32[32,128]{1,0:T(8,128)S(1)} %get-tuple-element.7, f32[32,128]{1,0:T(8,128)S(1)} %get-tuple-element.34, f32[32]{0:T(128)S(1)} %broadcast_multiply_fusion.3, f32[32]{0:T(128)S(1)} %copy-done.34), kind=kOutput, calls=%fused_computation.13 | convolution fusion | flops 270594048 | bytes 5276032 | tf_op jit(solution)/shard_map/dot_general | solution.py:258
  180.0 4.3 %fusion = bf16[256,4096]{1,0:T(8,128)(2,1)} fusion(f32[256,4096]{1,0:T(8,128)} %fusion.4, bf16[4096,128]{1,0:T(8,128)(2,1)S(1)} %copy-done, f32[256,128]{0,1:T(8,128)S(1)} %collective-permute-done.1, f32[256,128]{0,1:T(8,128)S(1)} %get-tuple-element.40, pred[]{:T(512)S(6)} %eq.91, f32[256,128]{0,1:T(8,128)S(1)} %get-tuple-element.5, ...), kind=kOutput, calls=%fused_computation.1 | convolution fusion | flops 270761984 | bytes 7866369 | tf_op jit(solution)/shard_map/dot_general | solution.py:258
  184.2 4.4 %all-to-all-start.5 = ((bf16[16,16,4096]{2,1,0:T(8,128)(2,1)}), bf16[16,16,4096]{2,1,0:T(8,128)(2,1)S(1)}, u32[]{:S(2)}, u32[]{:S(2)}) async-start(bf16[16,16,4096]{2,1,0:T(8,128)(2,1)} %bitcast.18), calls=%async_computation.5 | async-start | bytes 4194304 | tf_op jit(solution)/shard_map/all_to_all | solution.py:64
  188.6 1.4 slice_reduce_fusion.1
  190.7 23.1 %all-to-all-done.5 = bf16[16,16,4096]{2,1,0:T(8,128)(2,1)S(1)} async-done(((bf16[16,16,4096]{2,1,0:T(8,128)(2,1)}), bf16[16,16,4096]{2,1,0:T(8,128)(2,1)S(1)}, u32[]{:S(2)}, u32[]{:S(2)}) %all-to-all-start.5) | async-done | bytes 2097184 | tf_op jit(solution)/shard_map/all_to_all | solution.py:64
  214.6 1.0 fusion.2
  (207 shorter events, 22.5 us)
Async XLA Ops:
  0.6 41.2 %copy-start = (bf16[4096,128]{1,0:T(8,128)(2,1)S(1)}, bf16[4096,128]{1,0:T(8,128)(2,1)}, u32[]{:S(2)}) copy-start(bf16[4096,128]{1,0:T(8,128)(2,1)} %param.17) | copy-start | bytes 3145732
  4.9 10.2 %copy-start.35 = (f32[128]{0:T(128)S(1)}, f32[128]{0:T(128)}, u32[]{:S(2)}) copy-start(f32[128]{0:T(128)} %param.18) | copy-start | bytes 1540
  4.9 10.8 %copy-start.47 = (s32[1,32]{1,0:T(1,128)S(1)}, s32[1,32]{1,0:T(1,128)}, u32[]{:S(2)}) copy-start(s32[1,32]{1,0:T(1,128)} %param.12) | copy-start | bytes 388
  4.9 12.6 %copy-start.2 = (bf16[16,4096]{1,0:T(8,128)(2,1)S(1)}, bf16[16,4096]{1,0:T(8,128)(2,1)}, u32[]{:S(2)}) copy-start(bf16[16,4096]{1,0:T(8,128)(2,1)} %param.11) | copy-start | bytes 393220
  4.9 34.9 %all-to-all-start = ((bf16[16,16,4096]{2,1,0:T(8,128)(2,1)}), bf16[16,16,4096]{2,1,0:T(8,128)(2,1)S(1)}, u32[]{:S(2)}, u32[]{:S(2)}) async-start(bf16[16,16,4096]{2,1,0:T(8,128)(2,1)} %broadcast_in_dim.31), calls=%async_computation | async-start | bytes 4194304 | tf_op jit(solution)/shard_map/all_to_all | solution.py:64
  17.3 25.4 %copy-start.43 = (s32[16]{0:T(128)}, s32[16]{0:T(128)S(1)}, u32[]{:S(2)}) copy-start(s32[16]{0:T(128)S(1)} %iota_add_fusion) | copy-start | bytes 196
  17.4 25.3 %copy-start.30 = (s32[32]{0:T(128)}, s32[32]{0:T(128)S(1)}, u32[]{:S(2)}) copy-start(s32[32]{0:T(128)S(1)} %broadcast_add_fusion) | copy-start | bytes 388
  17.5 33.1 %copy-start.7 = (f32[256,64]{0,1:T(8,128)}, f32[256,64]{0,1:T(8,128)S(1)}, u32[]{:S(2)}) copy-start(f32[256,64]{0,1:T(8,128)S(1)} %broadcast_multiply_fusion) | copy-start | bytes 196612
  42.7 7.7 %collective-permute-start = (f32[256,128]{0,1:T(8,128)S(1)}, f32[256,128]{0,1:T(8,128)S(1)}, u32[]{:S(2)}, u32[]{:S(2)}) collective-permute-start(f32[256,128]{0,1:T(8,128)S(1)} %fusion.88), channel_id=1, source_target_pairs={{0,1},{1,0},{2,3},{3,2},{4,5},{5,4},{6,7},{7,6},{8,9},{9,8},{10,11... | collective-permute-start | bytes 393224 | tf_op jit(solution)/shard_map/ppermute | solution.py:17
  52.0 53.6 %copy-start.9 = (f32[32,256]{1,0:T(8,128)}, f32[32,256]{1,0:T(8,128)S(1)}, u32[]{:S(2)}) copy-start(f32[32,256]{1,0:T(8,128)S(1)} %get-tuple-element.36) | copy-start | bytes 98308
  52.0 53.6 %copy-start.39 = (f32[32]{0:T(128)}, f32[32]{0:T(128)S(1)}, u32[]{:S(2)}) copy-start(f32[32]{0:T(128)S(1)} %get-tuple-element.35) | copy-start | bytes 388
  53.3 12.7 %all-to-all-start.1 = ((bf16[16,32,256]{2,1,0:T(8,128)(2,1)}), bf16[16,32,256]{2,1,0:T(8,128)(2,1)S(1)}, u32[]{:S(2)}, u32[]{:S(2)}) async-start(bf16[16,32,256]{2,1,0:T(8,128)(2,1)} %bitcast.79), calls=%async_computation.1 | async-start | bytes 524288 | tf_op jit(solution)/shard_map/all_to_all | solution.py:64
  59.3 48.1 %copy-start.27 = (f32[256]{0:T(256)}, f32[256]{0:T(256)S(1)}, u32[]{:S(2)}) copy-start(f32[256]{0:T(256)S(1)} %dynamic_slice.30) | copy-start | bytes 3076
  66.0 39.5 %copy-start.11 = (f32[32,256]{1,0:T(8,128)}, f32[32,256]{1,0:T(8,128)S(1)}, u32[]{:S(2)}) copy-start(f32[32,256]{1,0:T(8,128)S(1)} %convert_reduce_fusion.1) | copy-start | bytes 98308
  109.6 19.6 %all-to-all-start.2 = ((f32[16,104,128]{2,1,0:T(8,128)}), f32[16,104,128]{2,1,0:T(8,128)S(1)}, u32[]{:S(2)}, u32[]{:S(2)}) async-start(f32[16,104,128]{2,1,0:T(8,128)} %pad_maximum_fusion), calls=%async_computation.2 | async-start | bytes 1703936 | tf_op jit(solution)/shard_map/all_to_all | solution.py:64
  129.2 13.1 %copy-start.6 = (bf16[256,256]{1,0:T(8,128)(2,1)S(1)}, bf16[256,256]{1,0:T(8,128)(2,1)}, u32[]{:S(2)}) copy-start(bf16[256,256]{1,0:T(8,128)(2,1)} %copy-done.5) | copy-start | bytes 393220
  135.5 16.0 %all-to-all-start.3 = ((bf16[16,128,128]{2,1,0:T(8,128)(2,1)}), bf16[16,128,128]{2,1,0:T(8,128)(2,1)}, u32[]{:S(2)}, u32[]{:S(2)}) async-start(bf16[16,128,128]{2,1,0:T(8,128)(2,1)} %broadcast_in_dim.40), calls=%async_computation.3 | async-start | bytes 1048576 | tf_op jit(solution)/shard_map/all_to_all | solution.py:64
  155.3 15.2 %copy-start.10 = (f32[32,256]{1,0:T(8,128)S(1)}, f32[32,256]{1,0:T(8,128)}, u32[]{:S(2)}) copy-start(f32[32,256]{1,0:T(8,128)} %copy-done.9) | copy-start | bytes 98308
  156.5 14.1 %copy-start.15 = (bf16[256,128]{0,1:T(8,128)(2,1)S(1)}, bf16[256,128]{0,1:T(8,128)(2,1)}, u32[]{:S(2)}) copy-start(bf16[256,128]{0,1:T(8,128)(2,1)} %copy-done.14) | copy-start | bytes 196612
  156.5 14.1 %copy-start.40 = (f32[32]{0:T(128)S(1)}, f32[32]{0:T(128)}, u32[]{:S(2)}) copy-start(f32[32]{0:T(128)} %copy-done.39) | copy-start | bytes 388
  156.5 14.4 %copy-start.17 = (bf16[256,128]{0,1:T(8,128)(2,1)S(1)}, bf16[256,128]{0,1:T(8,128)(2,1)}, u32[]{:S(2)}) copy-start(bf16[256,128]{0,1:T(8,128)(2,1)} %copy-done.16) | copy-start | bytes 196612
  156.5 14.5 %copy-start.25 = (bf16[32,128]{1,0:T(8,128)(2,1)S(1)}, bf16[32,128]{1,0:T(8,128)(2,1)}, u32[]{:S(2)}) copy-start(bf16[32,128]{1,0:T(8,128)(2,1)} %copy-done.24) | copy-start | bytes 24580
  156.6 14.9 %copy-start.20 = (f32[32,64]{1,0:T(8,128)S(1)}, f32[32,64]{1,0:T(8,128)}, u32[]{:S(2)}) copy-start(f32[32,64]{1,0:T(8,128)} %copy-done.19) | copy-start | bytes 24580
  156.6 14.8 %copy-start.34 = (f32[32]{0:T(128)S(1)}, f32[32]{0:T(128)}, u32[]{:S(2)}) copy-start(f32[32]{0:T(128)} %copy-done.33) | copy-start | bytes 388
  156.6 14.8 %copy-start.36 = (f32[128]{0:T(128)S(1)}, f32[128]{0:T(128)}, u32[]{:S(2)}) copy-start(f32[128]{0:T(128)} %param.18) | copy-start | bytes 1540
  156.6 15.1 %copy-start.8 = (f32[256,64]{0,1:T(8,128)S(1)}, f32[256,64]{0,1:T(8,128)}, u32[]{:S(2)}) copy-start(f32[256,64]{0,1:T(8,128)} %copy-done.7) | copy-start | bytes 196612
  156.6 15.1 %copy-start.23 = (f32[256]{0:T(256)S(1)}, f32[256]{0:T(256)}, u32[]{:S(2)}) copy-start(f32[256]{0:T(256)} %copy-done.22) | copy-start | bytes 3076
  156.6 15.1 %copy-start.42 = (f32[128]{0:T(128)S(1)}, f32[128]{0:T(128)}, u32[]{:S(2)}) copy-start(f32[128]{0:T(128)} %param.19) | copy-start | bytes 1540
  172.5 7.5 %collective-permute-start.1 = (f32[256,128]{0,1:T(8,128)S(1)}, f32[256,128]{0,1:T(8,128)S(1)}, u32[]{:S(2)}, u32[]{:S(2)}) collective-permute-start(f32[256,128]{0,1:T(8,128)S(1)} %get-tuple-element.39), channel_id=1, source_target_pairs={{0,1},{1,0},{2,3},{3,2},{4,5},{5,4},{6,7},{7,6},{8,9},{9,8},{10,11... | collective-permute-start | bytes 393224 | tf_op jit(solution)/shard_map/ppermute | solution.py:17
  184.2 29.5 %all-to-all-start.5 = ((bf16[16,16,4096]{2,1,0:T(8,128)(2,1)}), bf16[16,16,4096]{2,1,0:T(8,128)(2,1)S(1)}, u32[]{:S(2)}, u32[]{:S(2)}) async-start(bf16[16,16,4096]{2,1,0:T(8,128)(2,1)} %bitcast.18), calls=%async_computation.5 | async-start | bytes 4194304 | tf_op jit(solution)/shard_map/all_to_all | solution.py:64
  188.6 25.4 %copy-start.3 = (bf16[16,4096]{1,0:T(8,128)(2,1)S(1)}, bf16[16,4096]{1,0:T(8,128)(2,1)}, u32[]{:S(2)}) copy-start(bf16[16,4096]{1,0:T(8,128)(2,1)} %param.11) | copy-start | bytes 393220
  188.6 25.5 %copy-start.18 = (f32[4096]{0:T(1024)S(1)}, f32[4096]{0:T(1024)}, u32[]{:S(2)}) copy-start(f32[4096]{0:T(1024)} %param.15) | copy-start | bytes 49156
  (26 other events, 97.2 us)
where the time goes:
time: 218 us; the launch traced here: 217 us
  waiting for transfers between devices  74.1 us (34%)
  blocking collectives  51.1 us (23%)
  starting transfers between devices  37.9 us (17%)
  matrix products  16.9 us (8%)
  local copies, waits for them, and re-layouts  16.2 us (7%)
  other arithmetic  15.9 us (7%)
  between operations  4.59 us (2%)
    all_to_all x5, waiting for transfers between devices, exchange(): return lax.all_to_all(blocks, axis, 0, 0, tiled=True)  71.5 us
    all_gather x1, blocking collectives, on_device(): lax.all_gather(scaled.astype(jnp.bfloat16), 'dp', axis=0, tiled=True)  39.5 us
    all_to_all x5, starting transfers between devices, exchange(): return lax.all_to_all(blocks, axis, 0, 0, tiled=True)  29.7 us
    all_to_all x1, blocking collectives, exchange(): return lax.all_to_all(blocks, axis, 0, 0, tiled=True)  11.6 us
    ppermute x2, starting transfers between devices, swapped(): return lax.ppermute(value, axis, pairs)  8.13 us
  transfers between devices with their start and end apart: 7, of which 6 were waited for; matrix products, arithmetic and copies ran while one was open for 6% of the time, Pallas kernels for 0%

commit v1 on v0

--- a/solution.py
+++ b/solution.py
@@ -225,7 +225,10 @@
     resid = jnp.sum(arrived.astype(jnp.float32), axis=0)
     own_gain = lax.dynamic_slice_in_dim(out_gain, tensor_index * chunk, chunk)
     scaled = resid * own_gain
-    everyone = lax.all_gather(scaled.astype(jnp.bfloat16), "dp", axis=0, tiled=True)
+    everyone = jnp.concatenate(
+        lax.all_to_all(jnp.stack([scaled.astype(jnp.bfloat16)] * lax.axis_size("dp")), "dp", 0, 0),
+        axis=0,
+    )
     groups = lax.axis_size("dp")
     loss, d_embed, along, inverse = contrast(
         everyone.reshape(groups, sequences, chunk), own_gain, positives, negatives

time: 218 us -> 230 us (1.055)
  the two profiles are of different devices: /device:TPU:2 before, /device:TPU:64 now
where the time goes in v1:
time: 230 us; the launch traced here: 228 us
  waiting for transfers between devices  91.2 us (40%)
  blocking collectives  56.3 us (24%)
  starting transfers between devices  26.8 us (12%)
  matrix products  16.9 us (7%)
  local copies, waits for them, and re-layouts  16.6 us (7%)
  other arithmetic  15.9 us (7%)
  between operations  4.69 us (2%)
    all_to_all x5, waiting for transfers between devices, exchange(): return lax.all_to_all(blocks, axis, 0, 0, tiled=True)  86.3 us
    all_to_all x1, blocking collectives, on_device(): lax.all_to_all(jnp.stack([scaled.astype(jnp.bfloat16)] * lax.axis_size('d...  44.8 us
    all_to_all x5, starting transfers between devices, exchange(): return lax.all_to_all(blocks, axis, 0, 0, tiled=True)  22.3 us
    all_to_all x1, blocking collectives, exchange(): return lax.all_to_all(blocks, axis, 0, 0, tiled=True)  11.5 us
    ppermute x2, waiting for transfers between devices, swapped(): return lax.ppermute(value, axis, pairs)  4.9 us
  transfers between devices with their start and end apart: 7, of which 7 were waited for; matrix products, arithmetic and copies ran while one was open for 6% of the time, Pallas kernels for 0%

profile of v1, /device:TPU:64, one launch (start us, length us, event | category | flops | bytes accessed | tf_op | source)
XLA Modules:
  0.0 228.5 jit_solution(14501871206120959050)
XLA Ops:
  0.6 1.1 fusion.24
  2.3 1.0 fusion.20
  3.3 1.6 broadcast_in_dim.31
  4.9 7.2 %all-to-all-start = ((bf16[16,16,4096]{2,1,0:T(8,128)(2,1)}), bf16[16,16,4096]{2,1,0:T(8,128)(2,1)S(1)}, u32[]{:S(2)}, u32[]{:S(2)}) async-start(bf16[16,16,4096]{2,1,0:T(8,128)(2,1)} %broadcast_in_dim.31), calls=%async_computation | async-start | bytes 4194304 | tf_op jit(solution)/shard_map/all_to_all | solution.py:64
  15.2 1.1 fusion.53
  16.2 27.5 %all-to-all-done = bf16[16,16,4096]{2,1,0:T(8,128)(2,1)S(1)} async-done(((bf16[16,16,4096]{2,1,0:T(8,128)(2,1)}), bf16[16,16,4096]{2,1,0:T(8,128)(2,1)S(1)}, u32[]{:S(2)}, u32[]{:S(2)}) %all-to-all-start) | async-done | bytes 2097184 | tf_op jit(solution)/shard_map/all_to_all | solution.py:64
  43.8 2.0 multiply_reduce_fusion.6
  46.7 2.1 collective-permute-start
  49.0 4.6 %collective-permute-done = f32[256,128]{0,1:T(8,128)S(1)} collective-permute-done((f32[256,128]{0,1:T(8,128)S(1)}, f32[256,128]{0,1:T(8,128)S(1)}, u32[]{:S(2)}, u32[]{:S(2)}) %collective-permute-start) | collective-permute-done | bytes 131104 | tf_op jit(solution)/shard_map/ppermute | solution.py:17
  56.5 3.6 %all-to-all-start.1 = ((bf16[16,32,256]{2,1,0:T(8,128)(2,1)}), bf16[16,32,256]{2,1,0:T(8,128)(2,1)S(1)}, u32[]{:S(2)}, u32[]{:S(2)}) async-start(bf16[16,32,256]{2,1,0:T(8,128)(2,1)} %bitcast.78), calls=%async_computation.1 | async-start | bytes 524288 | tf_op jit(solution)/shard_map/all_to_all | solution.py:64
  60.8 7.9 %all-to-all-done.1 = bf16[16,32,256]{2,1,0:T(8,128)(2,1)S(1)} async-done(((bf16[16,32,256]{2,1,0:T(8,128)(2,1)}), bf16[16,32,256]{2,1,0:T(8,128)(2,1)S(1)}, u32[]{:S(2)}, u32[]{:S(2)}) %all-to-all-start.1) | async-done | bytes 262176 | tf_op jit(solution)/shard_map/all_to_all | solution.py:64
  68.9 44.8 %all_to_all.39 = bf16[32,32,256]{2,1,0:T(8,128)(2,1)S(1)} all-to-all(bf16[32,32,256]{2,1,0:T(8,128)(2,1)S(1)} %stack.2), channel_id=1, replica_groups=mesh['dp'=32,'tensor'=16] {'dp'}, dimensions={0} | all-to-all | bytes 1048576 | tf_op jit(solution)/shard_map/all_to_all | solution.py:229
  115.0 0.9 reshape_reshape.3
  115.9 2.1 pad_maximum_fusion
  118.1 3.6 %all-to-all-start.3 = ((f32[16,104,128]{2,1,0:T(8,128)}), f32[16,104,128]{2,1,0:T(8,128)S(1)}, u32[]{:S(2)}, u32[]{:S(2)}) async-start(f32[16,104,128]{2,1,0:T(8,128)} %pad_maximum_fusion), calls=%async_computation.3 | async-start | bytes 1703936 | tf_op jit(solution)/shard_map/all_to_all | solution.py:64
  124.8 14.3 %all-to-all-done.3 = f32[16,104,128]{2,1,0:T(8,128)S(1)} async-done(((f32[16,104,128]{2,1,0:T(8,128)}), f32[16,104,128]{2,1,0:T(8,128)S(1)}, u32[]{:S(2)}, u32[]{:S(2)}) %all-to-all-start.3) | async-done | bytes 852000 | tf_op jit(solution)/shard_map/all_to_all | solution.py:64
  139.4 0.9 fusion.51
  140.7 1.0 multiply_reduce_fusion.2
  144.4 0.9 broadcast_in_dim.40
  145.3 4.2 %all-to-all-start.4 = ((bf16[16,128,128]{2,1,0:T(8,128)(2,1)}), bf16[16,128,128]{2,1,0:T(8,128)(2,1)}, u32[]{:S(2)}, u32[]{:S(2)}) async-start(bf16[16,128,128]{2,1,0:T(8,128)(2,1)} %broadcast_in_dim.40), calls=%async_computation.4 | async-start | bytes 1048576 | tf_op jit(solution)/shard_map/all_to_all | solution.py:64
  151.1 10.6 %all-to-all-done.4 = bf16[16,128,128]{2,1,0:T(8,128)(2,1)} async-done(((bf16[16,128,128]{2,1,0:T(8,128)(2,1)}), bf16[16,128,128]{2,1,0:T(8,128)(2,1)}, u32[]{:S(2)}, u32[]{:S(2)}) %all-to-all-start.4) | async-done | bytes 524320 | tf_op jit(solution)/shard_map/all_to_all | solution.py:64
  161.7 0.9 slice.105
  163.9 1.0 slice.102
  165.6 1.2 fusion.25
  168.7 11.5 %all_to_all.40 = bf16[16,32,256]{2,1,0:T(8,128)(2,1)S(1)} all-to-all(bf16[16,32,256]{2,1,0:T(8,128)(2,1)S(1)} %broadcast_in_dim.41), channel_id=1, replica_groups=mesh['dp'=32,'tensor'=16] {'tensor'}, dimensions={0} | all-to-all | bytes 524288 | tf_op jit(solution)/shard_map/all_to_all | solution.py:64
  182.6 2.5 %collective-permute-start.1 = (f32[256,128]{0,1:T(8,128)S(1)}, f32[256,128]{0,1:T(8,128)S(1)}, u32[]{:S(2)}, u32[]{:S(2)}) collective-permute-start(f32[256,128]{0,1:T(8,128)S(1)} %get-tuple-element.39), channel_id=1, source_target_pairs={{0,1},{1,0},{2,3},{3,2},{4,5},{5,4},{6,7},{7,6},{8,9},{9,8},{10,11... | collective-permute-start | bytes 393224 | tf_op jit(solution)/shard_map/ppermute | solution.py:17
  185.1 4.1 %fusion.4 = f32[256,4096]{1,0:T(8,128)} fusion(bf16[4096,128]{1,0:T(8,128)(2,1)} %param.16, s32[32]{0:T(128)S(1)} %copy-done.31, f32[32,128]{1,0:T(8,128)S(1)} %get-tuple-element.7, f32[32,128]{1,0:T(8,128)S(1)} %get-tuple-element.34, f32[32]{0:T(128)S(1)} %broadcast_multiply_fusion.3, f32[32]{0:T(128)S(1)} %copy-done.34), kind=kOutput, calls=%fused_computation.13 | convolution fusion | flops 270594048 | bytes 5276032 | tf_op jit(solution)/shard_map/dot_general | solution.py:261
  189.5 4.3 %fusion = bf16[256,4096]{1,0:T(8,128)(2,1)} fusion(f32[256,4096]{1,0:T(8,128)} %fusion.4, bf16[4096,128]{1,0:T(8,128)(2,1)S(1)} %copy-done, f32[256,128]{0,1:T(8,128)S(1)} %collective-permute-done.1, f32[256,128]{0,1:T(8,128)S(1)} %get-tuple-element.40, pred[]{:T(512)S(6)} %eq.91, f32[256,128]{0,1:T(8,128)S(1)} %get-tuple-element.5, ...), kind=kOutput, calls=%fused_computation.1 | convolution fusion | flops 270761984 | bytes 7866369 | tf_op jit(solution)/shard_map/dot_general | solution.py:261
  193.8 3.7 %all-to-all-start.6 = ((bf16[16,16,4096]{2,1,0:T(8,128)(2,1)}), bf16[16,16,4096]{2,1,0:T(8,128)(2,1)S(1)}, u32[]{:S(2)}, u32[]{:S(2)}) async-start(bf16[16,16,4096]{2,1,0:T(8,128)(2,1)} %bitcast.17), calls=%async_computation.6 | async-start | bytes 4194304 | tf_op jit(solution)/shard_map/all_to_all | solution.py:64
  197.5 1.4 slice_reduce_fusion.1
  199.6 25.9 %all-to-all-done.6 = bf16[16,16,4096]{2,1,0:T(8,128)(2,1)S(1)} async-done(((bf16[16,16,4096]{2,1,0:T(8,128)(2,1)}), bf16[16,16,4096]{2,1,0:T(8,128)(2,1)S(1)}, u32[]{:S(2)}, u32[]{:S(2)}) %all-to-all-start.6) | async-done | bytes 2097184 | tf_op jit(solution)/shard_map/all_to_all | solution.py:64
  226.4 1.0 fusion.2
  (208 shorter events, 23.2 us)
Async XLA Ops:
  0.6 45.1 %copy-start = (bf16[4096,128]{1,0:T(8,128)(2,1)S(1)}, bf16[4096,128]{1,0:T(8,128)(2,1)}, u32[]{:S(2)}) copy-start(bf16[4096,128]{1,0:T(8,128)(2,1)} %param.17) | copy-start | bytes 3145732
  4.9 10.2 %copy-start.2 = (bf16[16,4096]{1,0:T(8,128)(2,1)S(1)}, bf16[16,4096]{1,0:T(8,128)(2,1)}, u32[]{:S(2)}) copy-start(bf16[16,4096]{1,0:T(8,128)(2,1)} %param.11) | copy-start | bytes 393220
  4.9 38.8 %all-to-all-start = ((bf16[16,16,4096]{2,1,0:T(8,128)(2,1)}), bf16[16,16,4096]{2,1,0:T(8,128)(2,1)S(1)}, u32[]{:S(2)}, u32[]{:S(2)}) async-start(bf16[16,16,4096]{2,1,0:T(8,128)(2,1)} %broadcast_in_dim.31), calls=%async_computation | async-start | bytes 4194304 | tf_op jit(solution)/shard_map/all_to_all | solution.py:64
  14.9 31.7 %copy-start.43 = (s32[16]{0:T(128)}, s32[16]{0:T(128)S(1)}, u32[]{:S(2)}) copy-start(s32[16]{0:T(128)S(1)} %iota_add_fusion) | copy-start | bytes 196
  15.1 31.6 %copy-start.30 = (s32[32]{0:T(128)}, s32[32]{0:T(128)S(1)}, u32[]{:S(2)}) copy-start(s32[32]{0:T(128)S(1)} %broadcast_add_fusion) | copy-start | bytes 388
  15.2 38.7 %copy-start.7 = (f32[256,64]{0,1:T(8,128)}, f32[256,64]{0,1:T(8,128)S(1)}, u32[]{:S(2)}) copy-start(f32[256,64]{0,1:T(8,128)S(1)} %broadcast_multiply_fusion) | copy-start | bytes 196612
  46.6 8.7 %copy-start.1 = (bf16[128,4096]{1,0:T(8,128)(2,1)S(1)}, bf16[128,4096]{1,0:T(8,128)(2,1)}, u32[]{:S(2)}) copy-start(bf16[128,4096]{1,0:T(8,128)(2,1)} %param.20) | copy-start | bytes 3145732
  46.6 8.7 %copy-start.4 = (f32[32,4096]{1,0:T(8,128)S(1)}, f32[32,4096]{1,0:T(8,128)}, u32[]{:S(2)}) copy-start(f32[32,4096]{1,0:T(8,128)} %fusion.53) | copy-start | bytes 1572868
  46.7 7.0 %collective-permute-start = (f32[256,128]{0,1:T(8,128)S(1)}, f32[256,128]{0,1:T(8,128)S(1)}, u32[]{:S(2)}, u32[]{:S(2)}) collective-permute-start(f32[256,128]{0,1:T(8,128)S(1)} %fusion.88), channel_id=1, source_target_pairs={{0,1},{1,0},{2,3},{3,2},{4,5},{5,4},{6,7},{7,6},{8,9},{9,8},{10,11... | collective-permute-start | bytes 393224 | tf_op jit(solution)/shard_map/ppermute | solution.py:17
  55.2 13.6 %copy-start.9 = (f32[32,256]{1,0:T(8,128)}, f32[32,256]{1,0:T(8,128)S(1)}, u32[]{:S(2)}) copy-start(f32[32,256]{1,0:T(8,128)S(1)} %get-tuple-element.36) | copy-start | bytes 98308
  55.2 13.6 %copy-start.39 = (f32[32]{0:T(128)}, f32[32]{0:T(128)S(1)}, u32[]{:S(2)}) copy-start(f32[32]{0:T(128)S(1)} %get-tuple-element.35) | copy-start | bytes 388
  56.5 12.2 %all-to-all-start.1 = ((bf16[16,32,256]{2,1,0:T(8,128)(2,1)}), bf16[16,32,256]{2,1,0:T(8,128)(2,1)S(1)}, u32[]{:S(2)}, u32[]{:S(2)}) async-start(bf16[16,32,256]{2,1,0:T(8,128)(2,1)} %bitcast.78), calls=%async_computation.1 | async-start | bytes 524288 | tf_op jit(solution)/shard_map/all_to_all | solution.py:64
  60.8 54.2 %copy-start.27 = (f32[256]{0:T(256)}, f32[256]{0:T(256)S(1)}, u32[]{:S(2)}) copy-start(f32[256]{0:T(256)S(1)} %dynamic_slice.30) | copy-start | bytes 3076
  68.8 44.9 %copy-start.11 = (f32[32,256]{1,0:T(8,128)}, f32[32,256]{1,0:T(8,128)S(1)}, u32[]{:S(2)}) copy-start(f32[32,256]{1,0:T(8,128)S(1)} %convert_reduce_fusion.1) | copy-start | bytes 98308
  118.1 21.0 %all-to-all-start.3 = ((f32[16,104,128]{2,1,0:T(8,128)}), f32[16,104,128]{2,1,0:T(8,128)S(1)}, u32[]{:S(2)}, u32[]{:S(2)}) async-start(f32[16,104,128]{2,1,0:T(8,128)} %pad_maximum_fusion), calls=%async_computation.3 | async-start | bytes 1703936 | tf_op jit(solution)/shard_map/all_to_all | solution.py:64
  139.1 11.7 %copy-start.6 = (bf16[256,256]{1,0:T(8,128)(2,1)S(1)}, bf16[256,256]{1,0:T(8,128)(2,1)}, u32[]{:S(2)}) copy-start(bf16[256,256]{1,0:T(8,128)(2,1)} %copy-done.5) | copy-start | bytes 393220
  145.3 16.3 %all-to-all-start.4 = ((bf16[16,128,128]{2,1,0:T(8,128)(2,1)}), bf16[16,128,128]{2,1,0:T(8,128)(2,1)}, u32[]{:S(2)}, u32[]{:S(2)}) async-start(bf16[16,128,128]{2,1,0:T(8,128)(2,1)} %broadcast_in_dim.40), calls=%async_computation.4 | async-start | bytes 1048576 | tf_op jit(solution)/shard_map/all_to_all | solution.py:64
  165.6 15.1 %copy-start.10 = (f32[32,256]{1,0:T(8,128)S(1)}, f32[32,256]{1,0:T(8,128)}, u32[]{:S(2)}) copy-start(f32[32,256]{1,0:T(8,128)} %copy-done.9) | copy-start | bytes 98308
  166.8 13.9 %copy-start.15 = (bf16[256,128]{0,1:T(8,128)(2,1)S(1)}, bf16[256,128]{0,1:T(8,128)(2,1)}, u32[]{:S(2)}) copy-start(bf16[256,128]{0,1:T(8,128)(2,1)} %copy-done.14) | copy-start | bytes 196612
  166.8 13.9 %copy-start.40 = (f32[32]{0:T(128)S(1)}, f32[32]{0:T(128)}, u32[]{:S(2)}) copy-start(f32[32]{0:T(128)} %copy-done.39) | copy-start | bytes 388
  166.8 14.3 %copy-start.17 = (bf16[256,128]{0,1:T(8,128)(2,1)S(1)}, bf16[256,128]{0,1:T(8,128)(2,1)}, u32[]{:S(2)}) copy-start(bf16[256,128]{0,1:T(8,128)(2,1)} %copy-done.16) | copy-start | bytes 196612
  166.8 14.4 %copy-start.25 = (bf16[32,128]{1,0:T(8,128)(2,1)S(1)}, bf16[32,128]{1,0:T(8,128)(2,1)}, u32[]{:S(2)}) copy-start(bf16[32,128]{1,0:T(8,128)(2,1)} %copy-done.24) | copy-start | bytes 24580
  166.8 14.7 %copy-start.20 = (f32[32,64]{1,0:T(8,128)S(1)}, f32[32,64]{1,0:T(8,128)}, u32[]{:S(2)}) copy-start(f32[32,64]{1,0:T(8,128)} %copy-done.19) | copy-start | bytes 24580
  166.8 14.7 %copy-start.34 = (f32[32]{0:T(128)S(1)}, f32[32]{0:T(128)}, u32[]{:S(2)}) copy-start(f32[32]{0:T(128)} %copy-done.33) | copy-start | bytes 388
  166.8 14.7 %copy-start.36 = (f32[128]{0:T(128)S(1)}, f32[128]{0:T(128)}, u32[]{:S(2)}) copy-start(f32[128]{0:T(128)} %param.18) | copy-start | bytes 1540
  166.8 15.0 %copy-start.8 = (f32[256,64]{0,1:T(8,128)S(1)}, f32[256,64]{0,1:T(8,128)}, u32[]{:S(2)}) copy-start(f32[256,64]{0,1:T(8,128)} %copy-done.7) | copy-start | bytes 196612
  166.8 15.0 %copy-start.23 = (f32[256]{0:T(256)S(1)}, f32[256]{0:T(256)}, u32[]{:S(2)}) copy-start(f32[256]{0:T(256)} %copy-done.22) | copy-start | bytes 3076
  166.9 15.0 %copy-start.42 = (f32[128]{0:T(128)S(1)}, f32[128]{0:T(128)}, u32[]{:S(2)}) copy-start(f32[128]{0:T(128)} %param.19) | copy-start | bytes 1540
  182.6 6.9 %collective-permute-start.1 = (f32[256,128]{0,1:T(8,128)S(1)}, f32[256,128]{0,1:T(8,128)S(1)}, u32[]{:S(2)}, u32[]{:S(2)}) collective-permute-start(f32[256,128]{0,1:T(8,128)S(1)} %get-tuple-element.39), channel_id=1, source_target_pairs={{0,1},{1,0},{2,3},{3,2},{4,5},{5,4},{6,7},{7,6},{8,9},{9,8},{10,11... | collective-permute-start | bytes 393224 | tf_op jit(solution)/shard_map/ppermute | solution.py:17
  193.8 31.7 %all-to-all-start.6 = ((bf16[16,16,4096]{2,1,0:T(8,128)(2,1)}), bf16[16,16,4096]{2,1,0:T(8,128)(2,1)S(1)}, u32[]{:S(2)}, u32[]{:S(2)}) async-start(bf16[16,16,4096]{2,1,0:T(8,128)(2,1)} %bitcast.17), calls=%async_computation.6 | async-start | bytes 4194304 | tf_op jit(solution)/shard_map/all_to_all | solution.py:64
  197.5 28.3 %copy-start.3 = (bf16[16,4096]{1,0:T(8,128)(2,1)S(1)}, bf16[16,4096]{1,0:T(8,128)(2,1)}, u32[]{:S(2)}) copy-start(bf16[16,4096]{1,0:T(8,128)(2,1)} %param.11) | copy-start | bytes 393220
  197.5 28.3 %copy-start.18 = (f32[4096]{0:T(1024)S(1)}, f32[4096]{0:T(1024)}, u32[]{:S(2)}) copy-start(f32[4096]{0:T(1024)} %param.15) | copy-start | bytes 49156
  (26 other events, 90.5 us)
